TPU v7x, 512 devices: a whole 4x4x16 slice. The times are simulated.
512 devices in a mesh: row: 16 (over x, z_lo), col: 32 (over z_hi, y, core).
Axes of the slice: x: 4, y: 4, z: 16 (z_hi: 4, z_lo: 4; z = z_hi * 4 + z_lo), core: 2. Of those that a mesh axis runs over, the one named last changes fastest.
Arguments:
- spectra: bfloat16 [2048, 2, 128, 128], P(('row', 'col')), may hold values from -3600 to 3600
- kept_windows: int32 [128], replicated, may hold values 0 or 1
Outputs:
- correlations: float32 [2048, 32, 64, 128], P('row', 'col')
All inputs are finite; a program needn't handle non-finite values.
Results may differ from a plain program's by a relative error of at most 0.0025.
Values may be sent and summed in bfloat16 or wider, within the bound.
A program may use at most 128 MiB of HBM per device.

v0:
```python
import math
import jax
import jax.numpy as jnp
from jax import lax
from jax.sharding import PartitionSpec as P

EPSILON = 1e-06


def make_lag_table(bins_count, windows):
    bin_ids = jnp.arange(bins_count, dtype=jnp.int32)
    phase_index = bin_ids[:, None] * bin_ids[None, :] % bins_count
    phases = phase_index.astype(jnp.float32) * (2.0 * math.pi / bins_count)
    norming = 1.0 / math.sqrt(bins_count * windows)
    return jnp.stack([jnp.cos(phases) * norming, -jnp.sin(phases) * norming], axis=1)


def partner_operand(col_rows):
    real_part = col_rows[:, 0]
    imag_part = col_rows[:, 1]
    re_half = jnp.concatenate([real_part, imag_part], axis=2)
    im_half = jnp.concatenate([-imag_part, real_part], axis=2)
    return jnp.concatenate([re_half, im_half], axis=0)


def cross_lags(first_rows, partner, lag_table):
    first_half = jnp.concatenate([first_rows[:, 0], first_rows[:, 1]], axis=2)
    stacks = lax.dot_general(
        first_half, partner, (((2,), (2,)), ((1,), (1,))), preferred_element_type=jnp.float32
    )
    partners_count = partner.shape[0] // 2
    stacks = stacks.reshape(stacks.shape[0], stacks.shape[1], 2, partners_count)
    return jnp.einsum("fmps,fpk->msk", stacks, lag_table, precision=lax.Precision.HIGHEST)


def body(spectra, kept_windows):
    bins_count = spectra.shape[2]
    windows = spectra.shape[3]
    own_float = spectra.astype(jnp.float32)
    partial_energy = jnp.sum(own_float * own_float, axis=(0, 1, 2))
    channels = spectra.shape[0] * lax.axis_size("row") * lax.axis_size("col")
    energy_sum = lax.psum(partial_energy, ("row", "col"))
    energy = energy_sum / (channels * 2 * bins_count) + EPSILON
    factor = kept_windows.astype(jnp.float32) / energy
    column_block = lax.all_gather(spectra, "row", axis=0, tiled=True)
    partner = partner_operand(column_block)
    lag_table = make_lag_table(bins_count, windows)
    row_block = lax.all_gather(spectra, "col", axis=0, tiled=True)
    lag_rows = cross_lags(
        (row_block.astype(jnp.float32) * factor).astype(jnp.bfloat16), partner, lag_table
    )
    return lag_rows[:, None]


def solution(mesh):
    placed = (P(("row", "col"), None, None, None), P())
    return jax.shard_map(
        body, mesh=mesh, in_specs=placed, out_specs=P("row", "col", None, None), check_vma=False
    )
```

profile of v0, /device:TPU:1, one launch (start us, length us, event | category | flops | bytes accessed | tf_op | source)
XLA Modules:
  0.0 314.2 jit_solution(12809178669511933960)
XLA Ops:
  6.5 0.0 all-gather.5.cloned.1.call-start
  6.5 0.7 all-gather.5.cloned.1.call-update
  7.3 0.0 all-gather.3.cloned.1.call-start
  7.3 0.7 all-gather.3.cloned.1.call-update
  8.0 1.1 multiply_reduce_fusion
  9.1 112.5 %psum.7 = f32[128]{0:T(128)S(1)} all-reduce(f32[128]{0:T(128)S(1)} %multiply_reduce_fusion), channel_id=1, replica_groups=mesh['row'=16,'col'=32] {'row','col'}, use_global_device_ids=true, to_apply=%region_1.0 | all-reduce | flops 128 | bytes 1024 | tf_op jit(solution)/shard_map/psum | solution.py:42
  121.6 0.3 negate_multiply_fusion
  121.9 0.7 add_divide_fusion
  122.6 1.0 all-gather.5.cloned.1.call-done
  123.6 2.7 fusion.27
  126.3 2.9 fusion.26
  129.3 4.6 %copy_bitcast_fusion = (bf16[64,128,128]{2,0,1:T(8,128)(2,1)}, bf16[64,128,128]{2,0,1:T(8,128)(2,1)}) fusion(bf16[64,1,128,128]{3,2,1,0:T(8,128)(2,1)S(1)} %get-tuple-element.7, bf16[64,1,128,128]{3,2,1,0:T(8,128)(2,1)S(1)} %get-tuple-element.8), kind=kLoop, calls=%fused_computation.17 | loop fusion | bytes 8388608 | tf_op jit(solution)/shard_map/squeeze | solution.py:20
  133.9 126.8 %all-gather.3.cloned.1.call-done = bf16[128,2,128,128]{3,2,1,0:T(8,128)(2,1)} async-done(((bf16[4,2,128,128]{3,2,1,0:T(8,128)(2,1)}), bf16[128,2,128,128]{3,2,1,0:T(8,128)(2,1)}) %all-gather.3.cloned.1.call-update) | async-done | bytes 8388624 | tf_op jit(solution)/shard_map/all_gather | solution.py:48
  260.7 12.0 %multiply_convert_fusion = bf16[128,2,128,128]{3,0,2,1:T(8,128)(2,1)} fusion(bf16[128,2,128,128]{3,2,1,0:T(8,128)(2,1)} %all-gather.3.cloned.1.call-done, f32[128]{0:T(128)S(1)} %add_divide_fusion), kind=kLoop, calls=%fused_computation | loop fusion | flops 12582912 | bytes 16777728 | tf_op jit(solution)/shard_map/convert_element_type | solution.py:50
  272.8 6.1 %slice_bitcast_fusion.1 = (bf16[128,128,128]{2,0,1:T(8,128)(2,1)}, bf16[128,128,128]{2,0,1:T(8,128)(2,1)}) fusion(bf16[128,2,128,128]{3,0,2,1:T(8,128)(2,1)} %multiply_convert_fusion), kind=kLoop, calls=%fused_computation.15 | loop fusion | bytes 16777216 | tf_op jit(solution)/shard_map/squeeze | solution.py:27
  278.9 7.1 %fusion = f32[128,128,128]{1,2,0:T(8,128)S(1)} fusion(bf16[128,128,128]{2,0,1:T(8,128)(2,1)} %get-tuple-element.6, bf16[128,128,128]{2,0,1:T(8,128)(2,1)} %get-tuple-element.5, bf16[64,128,128]{2,0,1:T(8,128)(2,1)} %get-tuple-element.10, bf16[64,128,128]{2,0,1:T(8,128)(2,1)} %fusion.26, bf16[64,128,128]{2,0,1:T(8,128)(2,1)} %get-tuple-element.9), kind=kOutput, calls=%fused_computation.1 | convolution fusion | flops 1124073472 | bytes 23068672 | tf_op jit(solution)/shard_map/dot_general | solution.py:28
  286.0 16.9 %fusion.13 = f32[128,1,64,128]{3,0,2,1:T(8,128)S(1)} fusion(f32[128,128,2,64]{1,3,2,0:T(8,128)S(1)} %bitcast.18, f32[128,1,128]{2,0,1:T(8,128)S(1)} %get-tuple-element.11, f32[128,1,128]{2,0,1:T(8,128)S(1)} %get-tuple-element.12), kind=kOutput, calls=%fused_computation.16 | convolution fusion | flops 3221258240 | bytes 12713984 | tf_op jit(solution)/shard_map/fmps,fpk->msk/dot_general | solution.py:33
  302.9 4.4 %copy.11 = f32[128,1,64,128]{3,2,1,0:T(8,128)} copy(f32[128,1,64,128]{3,0,2,1:T(8,128)S(1)} %fusion.13) | data formatting | bytes 8388608 | tf_op jit(solution)/shard_map/broadcast_in_dim | solution.py:52
Async XLA Ops:
  6.5 117.1 %all-gather.5.cloned.1.call-start = ((), (), s32[]{:S(2)}) async-start(), calls=%async_computation.1 | async-start | bytes 4456448 | tf_op jit(solution)/shard_map/all_gather | solution.py:45
  7.3 253.5 %all-gather.3.cloned.1.call-start = ((), (), s32[]{:S(2)}) async-start(), calls=%async_computation | async-start | bytes 8650752 | tf_op jit(solution)/shard_map/all_gather | solution.py:48
Sparse Core Ops, SparseCore 0:
  9.4 114.1 all-gather.4
  126.7 133.9 all-gather.2
where the time goes:
time: 314 us
  waiting for transfers between devices  129 us (41%)
  blocking collectives  113 us (36%)
  matrix products  24 us (8%)
  local copies, waits for them, and re-layouts  17.9 us (6%)
  other arithmetic  17 us (5%)
  between operations  13.4 us (4%)
    all_gather x1, waiting for transfers between devices, body(): row_block = lax.all_gather(spectra, 'col', axis=0, tiled=True)  127 us
    psum x1, blocking collectives, body(): energy_sum = lax.psum(partial_energy, ('row', 'col'))  113 us
    dot_general x1, matrix products, cross_lags(): jnp.einsum('fmps,fpk->msk', stacks, lag_table, precision=lax.Precision.HI...  16.9 us
    convert_element_type x1, other arithmetic, body(): (row_block.astype(jnp.float32) * factor).astype(jnp.bfloat16)  12 us
    dot_general x1, matrix products, cross_lags(): lax.dot_general(first_half, partner, (((2,), (2,)), ((1,), (1,))), prefer...  7.12 us
  transfers between devices with their start and end apart: 2, of which 2 were waited for; matrix products, arithmetic and copies ran while one was open for 4% of the time, Pallas kernels for 0%

commit v1 on v0

--- a/solution.py
+++ b/solution.py
@@ -45,7 +45,9 @@
     column_block = lax.all_gather(spectra, "row", axis=0, tiled=True)
     partner = partner_operand(column_block)
     lag_table = make_lag_table(bins_count, windows)
-    row_block = lax.all_gather(spectra, "col", axis=0, tiled=True)
+    row_block = jnp.concatenate(
+        lax.all_to_all(jnp.stack([spectra] * lax.axis_size("col")), "col", 0, 0), axis=0
+    )
     lag_rows = cross_lags(
         (row_block.astype(jnp.float32) * factor).astype(jnp.bfloat16), partner, lag_table
     )

time: 314 us -> 654 us (2.08)
  blocking collectives: 113 us -> 518 us
  waiting for transfers between devices: 129 us -> 0.7 us
  other arithmetic: 17 us -> 41.5 us
  starting transfers between devices: 0.04 us -> 19.6 us
  local copies, waits for them, and re-layouts: 17.9 us -> 33.1 us
    psum x1, blocking collectives: 113 us -> 518 us  [body(): energy_sum = lax.psum(partial_energy, ('row', 'col'))]
    all_gather x1 -> x0, waiting for transfers between devices: 127 us -> none  [body(): row_block = lax.all_gather(spectra, 'col', axis=0, tiled=True)]
    all_to_all x0 -> x1, starting transfers between devices: none -> 19.6 us  [body(): lax.all_to_all(jnp.stack([spectra] * lax.axis_size('col')), 'col', 0, 0)]
    convert_element_type x1, other arithmetic: 12 us -> 26.9 us  [body(): (row_block.astype(jnp.float32) * factor).astype(jnp.bfloat16)]
    convert_element_type x0 -> x1, other arithmetic: none -> 11.2 us  [body(): row_block.astype(jnp.float32) * factor]
    all_to_all x0 -> x1, local copies, waits for them, and re-layouts: none -> 8.97 us  [body(): lax.all_to_all(jnp.stack([spectra] * lax.axis_size('col')), 'col', 0, 0)]
    another operation x0 -> x1, local copies, waits for them, and re-layouts: none -> 7.27 us  [body(): jnp.stack([spectra] * lax.axis_size('col'))]
  transfers between devices with their start and end apart: 2 -> 2, of which waited for: 2 -> 0; matrix products, arithmetic and copies ran while one was open for 4% -> 2% of each run, Pallas kernels for 0% -> 0%
where the time goes in v1:
time: 654 us; the launch traced here: 651 us
  blocking collectives  518 us (79%)
  other arithmetic  41.5 us (6%)
  local copies, waits for them, and re-layouts  33.1 us (5%)
  matrix products  24 us (4%)
  starting transfers between devices  19.6 us (3%)
  between operations  13.7 us (2%)
    psum x1, blocking collectives, body(): energy_sum = lax.psum(partial_energy, ('row', 'col'))  518 us
    convert_element_type x1, other arithmetic, body(): (row_block.astype(jnp.float32) * factor).astype(jnp.bfloat16)  26.9 us
    all_to_all x1, starting transfers between devices, body(): lax.all_to_all(jnp.stack([spectra] * lax.axis_size('col')), 'col', 0, 0)  19.6 us
    dot_general x1, matrix products, cross_lags(): jnp.einsum('fmps,fpk->msk', stacks, lag_table, precision=lax.Precision.HI...  16.9 us
  transfers between devices with their start and end apart: 2, of which 0 were waited for; matrix products, arithmetic and copies ran while one was open for 2% of the time, Pallas kernels for 0%

profile of v1, /device:TPU:1, one launch (start us, length us, event | category | flops | bytes accessed | tf_op | source)
XLA Modules:
  0.0 650.9 jit_solution(10861820942700473595)
XLA Ops:
  6.5 1.2 copy.13
  7.7 7.3 %stack.4 = bf16[32,4,2,128,128]{4,1,3,2,0:T(4,128)(2,1)} broadcast(bf16[4,2,128,128]{3,0,2,1:T(4,128)(2,1)S(1)} %copy.13), dimensions={1,2,3,4} | broadcast | bytes 8650752 | tf_op jit(solution)/shard_map/stack | solution.py:49
  15.0 0.0 copy-start
  15.0 0.0 copy-start.1
  15.0 19.6 %all-to-all-start = ((bf16[32,4,2,128,128]{4,1,3,2,0:T(4,128)(2,1)}), bf16[32,4,2,128,128]{4,1,3,2,0:T(4,128)(2,1)}, u32[]{:S(2)}, u32[]{:S(2)}) async-start(bf16[32,4,2,128,128]{4,1,3,2,0:T(4,128)(2,1)} %stack.4), calls=%async_computation | async-start | bytes 16777216 | tf_op jit(solution)/shard_map/all_to_all | solution.py:49
  34.5 0.0 all-gather.2.cloned.1.call-start
  34.6 0.7 all-gather.2.cloned.1.call-update
  35.3 0.0 copy-done
  35.3 0.2 multiply_reduce_fusion
  35.4 518.3 %psum.7 = f32[128]{0:T(128)S(1)} all-reduce(f32[128]{0:T(128)S(1)} %multiply_reduce_fusion), channel_id=1, replica_groups=mesh['row'=16,'col'=32] {'row','col'}, use_global_device_ids=true, to_apply=%region_1.0 | all-reduce | flops 128 | bytes 1024 | tf_op jit(solution)/shard_map/psum | solution.py:42
  553.7 0.3 negate_multiply_fusion
  554.0 0.0 copy-done.1
  554.0 0.0 all-gather.2.cloned.1.call-done
  554.1 2.7 fusion.28
  556.8 2.9 fusion.27
  559.7 4.7 copy_bitcast_fusion
  564.4 0.0 all-to-all-done
  564.4 9.0 %copy.14 = bf16[32,4,2,128,128]{4,3,2,1,0:T(8,128)(2,1)} copy(bf16[32,4,2,128,128]{4,1,3,2,0:T(4,128)(2,1)} %all-to-all-done) | data formatting | bytes 16777216 | tf_op jit(solution)/shard_map/all_to_all | solution.py:49
  573.4 11.2 %bitcast_convert_fusion = f32[128,2,128,128]{3,2,1,0:T(8,128)} fusion(bf16[32,4,2,128,128]{4,3,2,1,0:T(8,128)(2,1)} %copy.14), kind=kLoop, calls=%fused_computation.13 | loop fusion | flops 4194304 | bytes 25165824 | tf_op jit(solution)/shard_map/convert_element_type | solution.py:52
  584.6 26.9 %fusion = bf16[128,2,128,128]{3,0,2,1:T(8,128)(2,1)S(1)} fusion(f32[128,2,128,128]{3,2,1,0:T(8,128)} %bitcast_convert_fusion, f32[128]{0:T(128)S(1)} %add_divide_fusion), kind=kLoop, calls=%fused_computation.1 | loop fusion | flops 8388608 | bytes 25166336 | tf_op jit(solution)/shard_map/convert_element_type | solution.py:52
  611.5 3.9 slice_bitcast_fusion.1
  615.4 7.1 %fusion.1 = f32[128,128,128]{1,2,0:T(8,128)S(1)} fusion(bf16[128,128,128]{2,0,1:T(8,128)(2,1)} %get-tuple-element.6, bf16[128,128,128]{2,0,1:T(8,128)(2,1)} %get-tuple-element.5, bf16[64,128,128]{2,0,1:T(8,128)(2,1)} %get-tuple-element.10, bf16[64,128,128]{2,0,1:T(8,128)(2,1)} %fusion.27, bf16[64,128,128]{2,0,1:T(8,128)(2,1)} %get-tuple-element.9), kind=kOutput, calls=%fused_computation.2 | convolution fusion | flops 1124073472 | bytes 23068672 | tf_op jit(solution)/shard_map/dot_general | solution.py:28
  622.5 16.9 %fusion.14 = f32[128,1,64,128]{3,0,2,1:T(8,128)S(1)} fusion(f32[128,128,2,64]{1,3,2,0:T(8,128)S(1)} %bitcast.21, f32[128,1,128]{2,0,1:T(8,128)S(1)} %get-tuple-element.11, f32[128,1,128]{2,0,1:T(8,128)S(1)} %get-tuple-element.12), kind=kOutput, calls=%fused_computation.18 | convolution fusion | flops 3221258240 | bytes 12713984 | tf_op jit(solution)/shard_map/fmps,fpk->msk/dot_general | solution.py:33
  639.4 4.4 copy.19
  (1 shorter events, 0.0 us)
Async XLA Ops:
  15.0 20.3 %copy-start = (bf16[4,2,128,128]{3,2,1,0:T(8,128)(2,1)S(1)}, bf16[4,2,128,128]{3,2,1,0:T(8,128)(2,1)}, u32[]{:S(2)}) copy-start(bf16[4,2,128,128]{3,2,1,0:T(8,128)(2,1)} %param.2) | copy-start | bytes 786436
  15.0 539.0 %copy-start.1 = (s32[128]{0:T(128)S(1)}, s32[128]{0:T(128)}, u32[]{:S(2)}) copy-start(s32[128]{0:T(128)} %param.3) | copy-start | bytes 1540
  15.0 549.4 %all-to-all-start = ((bf16[32,4,2,128,128]{4,1,3,2,0:T(4,128)(2,1)}), bf16[32,4,2,128,128]{4,1,3,2,0:T(4,128)(2,1)}, u32[]{:S(2)}, u32[]{:S(2)}) async-start(bf16[32,4,2,128,128]{4,1,3,2,0:T(4,128)(2,1)} %stack.4), calls=%async_computation | async-start | bytes 16777216 | tf_op jit(solution)/shard_map/all_to_all | solution.py:49
  34.5 519.5 %all-gather.2.cloned.1.call-start = ((), (), s32[]{:S(2)}) async-start(), calls=%async_computation.1 | async-start | bytes 4456448 | tf_op jit(solution)/shard_map/all_gather | solution.py:45
Sparse Core Ops, SparseCore 0:
  37.5 370.5 all-gather.1

commit v2 on v0

--- a/solution.py
+++ b/solution.py
@@ -39,7 +39,7 @@
     own_float = spectra.astype(jnp.float32)
     partial_energy = jnp.sum(own_float * own_float, axis=(0, 1, 2))
     channels = spectra.shape[0] * lax.axis_size("row") * lax.axis_size("col")
-    energy_sum = lax.psum(partial_energy, ("row", "col"))
+    energy_sum = lax.psum(lax.psum(partial_energy, "row"), "col")
     energy = energy_sum / (channels * 2 * bins_count) + EPSILON
     factor = kept_windows.astype(jnp.float32) / energy
     column_block = lax.all_gather(spectra, "row", axis=0, tiled=True)

time: 314 us -> 314 us (level)
  waiting for transfers between devices: 129 us -> 107 us
  blocking collectives: 113 us -> 134 us
    psum x1 -> x2, blocking collectives: 113 us -> 134 us  [body(): energy_sum = lax.psum(lax.psum(partial_energy, 'row'), 'col')]
    all_gather x1, waiting for transfers between devices: 127 us -> 106 us  [body(): row_block = lax.all_gather(spectra, 'col', axis=0, tiled=True)]
  transfers between devices with their start and end apart: 2 -> 2, of which waited for: 2 -> 1; matrix products, arithmetic and copies ran while one was open for 4% -> 4% of each run, Pallas kernels for 0% -> 0%
where the time goes in v2:
time: 314 us
  blocking collectives  134 us (43%)
  waiting for transfers between devices  107 us (34%)
  matrix products  24.2 us (8%)
  local copies, waits for them, and re-layouts  17.9 us (6%)
  other arithmetic  17 us (5%)
  between operations  13.4 us (4%)
    psum x2, blocking collectives, body(): energy_sum = lax.psum(lax.psum(partial_energy, 'row'), 'col')  134 us
    all_gather x1, waiting for transfers between devices, body(): row_block = lax.all_gather(spectra, 'col', axis=0, tiled=True)  106 us
    dot_general x1, matrix products, cross_lags(): jnp.einsum('fmps,fpk->msk', stacks, lag_table, precision=lax.Precision.HI...  16.9 us
    convert_element_type x1, other arithmetic, body(): (row_block.astype(jnp.float32) * factor).astype(jnp.bfloat16)  12 us
    dot_general x1, matrix products, cross_lags(): lax.dot_general(first_half, partner, (((2,), (2,)), ((1,), (1,))), prefer...  7.28 us
  transfers between devices with their start and end apart: 2, of which 1 were waited for; matrix products, arithmetic and copies ran while one was open for 4% of the time, Pallas kernels for 0%

profile of v2, /device:TPU:1, one launch (start us, length us, event | category | flops | bytes accessed | tf_op | source)
XLA Modules:
  0.0 314.0 jit_solution(16224193166396196249)
XLA Ops:
  6.5 0.0 all-gather.5.cloned.1.call-start
  6.5 0.7 all-gather.5.cloned.1.call-update
  7.3 0.0 all-gather.3.cloned.1.call-start
  7.3 0.7 all-gather.3.cloned.1.call-update
  8.0 1.1 multiply_reduce_fusion
  9.1 39.4 %psum.14 = f32[128]{0:T(128)S(1)} all-reduce(f32[128]{0:T(128)S(1)} %multiply_reduce_fusion), channel_id=1, replica_groups=mesh['row'=16,'col'=32] {'row'}, use_global_device_ids=true, to_apply=%region_1.0 | all-reduce | flops 128 | bytes 1024 | tf_op jit(solution)/shard_map/psum | solution.py:42
  48.5 94.9 %psum.15 = f32[128]{0:T(128)S(1)} all-reduce(f32[128]{0:T(128)S(1)} %psum.14), channel_id=1, replica_groups=mesh['row'=16,'col'=32] {'col'}, use_global_device_ids=true, to_apply=%region_2.0 | all-reduce | flops 128 | bytes 1024 | tf_op jit(solution)/shard_map/psum | solution.py:42
  143.4 0.3 negate_multiply_fusion
  143.7 0.7 add_divide_fusion
  144.3 0.0 all-gather.5.cloned.1.call-done
  144.3 2.7 fusion.27
  147.1 2.9 fusion.26
  150.0 4.6 %copy_bitcast_fusion = (bf16[64,128,128]{2,0,1:T(8,128)(2,1)}, bf16[64,128,128]{2,0,1:T(8,128)(2,1)}) fusion(bf16[64,1,128,128]{3,2,1,0:T(8,128)(2,1)S(1)} %get-tuple-element.7, bf16[64,1,128,128]{3,2,1,0:T(8,128)(2,1)S(1)} %get-tuple-element.8), kind=kLoop, calls=%fused_computation.17 | loop fusion | bytes 8388608 | tf_op jit(solution)/shard_map/squeeze | solution.py:20
  154.6 105.7 %all-gather.3.cloned.1.call-done = bf16[128,2,128,128]{3,2,1,0:T(8,128)(2,1)} async-done(((bf16[4,2,128,128]{3,2,1,0:T(8,128)(2,1)}), bf16[128,2,128,128]{3,2,1,0:T(8,128)(2,1)}) %all-gather.3.cloned.1.call-update) | async-done | bytes 8388624 | tf_op jit(solution)/shard_map/all_gather | solution.py:48
  260.4 12.0 %multiply_convert_fusion = bf16[128,2,128,128]{3,0,2,1:T(8,128)(2,1)} fusion(bf16[128,2,128,128]{3,2,1,0:T(8,128)(2,1)} %all-gather.3.cloned.1.call-done, f32[128]{0:T(128)S(1)} %add_divide_fusion), kind=kLoop, calls=%fused_computation | loop fusion | flops 12582912 | bytes 16777728 | tf_op jit(solution)/shard_map/convert_element_type | solution.py:50
  272.4 6.1 %slice_bitcast_fusion.1 = (bf16[128,128,128]{2,0,1:T(8,128)(2,1)}, bf16[128,128,128]{2,0,1:T(8,128)(2,1)}) fusion(bf16[128,2,128,128]{3,0,2,1:T(8,128)(2,1)} %multiply_convert_fusion), kind=kLoop, calls=%fused_computation.15 | loop fusion | bytes 16777216 | tf_op jit(solution)/shard_map/squeeze | solution.py:27
  278.5 7.3 %fusion = f32[128,128,128]{1,2,0:T(8,128)S(1)} fusion(bf16[128,128,128]{2,0,1:T(8,128)(2,1)} %get-tuple-element.6, bf16[128,128,128]{2,0,1:T(8,128)(2,1)} %get-tuple-element.5, bf16[64,128,128]{2,0,1:T(8,128)(2,1)} %get-tuple-element.10, bf16[64,128,128]{2,0,1:T(8,128)(2,1)} %fusion.26, bf16[64,128,128]{2,0,1:T(8,128)(2,1)} %get-tuple-element.9), kind=kOutput, calls=%fused_computation.1 | convolution fusion | flops 1124073472 | bytes 23068672 | tf_op jit(solution)/shard_map/dot_general | solution.py:28
  285.8 16.9 %fusion.13 = f32[128,1,64,128]{3,0,2,1:T(8,128)S(1)} fusion(f32[128,128,2,64]{1,3,2,0:T(8,128)S(1)} %bitcast.18, f32[128,1,128]{2,0,1:T(8,128)S(1)} %get-tuple-element.11, f32[128,1,128]{2,0,1:T(8,128)S(1)} %get-tuple-element.12), kind=kOutput, calls=%fused_computation.16 | convolution fusion | flops 3221258240 | bytes 12713984 | tf_op jit(solution)/shard_map/fmps,fpk->msk/dot_general | solution.py:33
  302.7 4.4 %copy.11 = f32[128,1,64,128]{3,2,1,0:T(8,128)} copy(f32[128,1,64,128]{3,0,2,1:T(8,128)S(1)} %fusion.13) | data formatting | bytes 8388608 | tf_op jit(solution)/shard_map/broadcast_in_dim | solution.py:52
Async XLA Ops:
  6.5 137.8 %all-gather.5.cloned.1.call-start = ((), (), s32[]{:S(2)}) async-start(), calls=%async_computation.1 | async-start | bytes 4456448 | tf_op jit(solution)/shard_map/all_gather | solution.py:45
  7.3 253.1 %all-gather.3.cloned.1.call-start = ((), (), s32[]{:S(2)}) async-start(), calls=%async_computation | async-start | bytes 8650752 | tf_op jit(solution)/shard_map/all_gather | solution.py:48
Sparse Core Ops, SparseCore 0:
  9.4 114.7 all-gather.4
  127.4 132.9 all-gather.2

commit v3 on v0

--- a/solution.py
+++ b/solution.py
@@ -39,7 +39,7 @@
     own_float = spectra.astype(jnp.float32)
     partial_energy = jnp.sum(own_float * own_float, axis=(0, 1, 2))
     channels = spectra.shape[0] * lax.axis_size("row") * lax.axis_size("col")
-    energy_sum = lax.psum(partial_energy, ("row", "col"))
+    energy_sum = jnp.sum(lax.all_gather(partial_energy, ("row", "col")), axis=0)
     energy = energy_sum / (channels * 2 * bins_count) + EPSILON
     factor = kept_windows.astype(jnp.float32) / energy
     column_block = lax.all_gather(spectra, "row", axis=0, tiled=True)

time: 314 us -> 890 us (2.83)
  the two profiles are of different devices: /device:TPU:1 before, /device:TPU:35 now
where the time goes in v3:
time: 890 us; the launch traced here: 881 us
  blocking collectives  794 us (89%)
  other arithmetic  29.5 us (3%)
  matrix products  24 us (3%)
  local copies, waits for them, and re-layouts  17.9 us (2%)
  between operations  13.8 us (2%)
    all_gather x1, blocking collectives, body(): energy_sum = jnp.sum(lax.all_gather(partial_energy, ('row', 'col')), axis=0)  794 us
    convert_element_type x1, other arithmetic, body(): (row_block.astype(jnp.float32) * factor).astype(jnp.bfloat16)  23.9 us
  transfers between devices with their start and end apart: 2, of which 0 were waited for; matrix products, arithmetic and copies ran while one was open for 1% of the time, Pallas kernels for 0%

profile of v3, /device:TPU:35, one launch (start us, length us, event | category | flops | bytes accessed | tf_op | source)
XLA Modules:
  0.0 880.8 jit_solution(14841206751318089038)
XLA Ops:
  6.5 0.0 all-gather.7.cloned.1.call-start
  6.5 0.7 all-gather.7.cloned.1.call-update
  7.3 0.0 all-gather.5.cloned.1.call-start
  7.3 0.7 all-gather.5.cloned.1.call-update
  8.0 1.1 multiply_reduce_fusion
  9.1 794.2 %all-gather.1 = f32[512,1,128]{2,1,0:T(1,128)S(1)} all-gather(f32[1,1,128]{2,1,0:T(1,128)S(1)} %bitcast.20), channel_id=2, replica_groups=mesh['row'=16,'col'=32] {'row','col'}, dimensions={0}, use_global_device_ids=true | all-gather | bytes 262656 | tf_op jit(solution)/shard_map/all_gather | solution.py:42
  803.3 0.6 reduce_sum.19
  803.8 0.3 negate_multiply_fusion
  804.1 0.7 add_divide_fusion
  804.8 0.0 all-gather.7.cloned.1.call-done
  804.8 2.7 fusion.27
  807.5 2.9 fusion.26
  810.5 4.6 copy_bitcast_fusion
  815.1 0.0 all-gather.5.cloned.1.call-done
  815.1 23.9 %multiply_convert_fusion = bf16[128,2,128,128]{3,0,2,1:T(8,128)(2,1)} fusion(bf16[128,2,128,128]{3,2,1,0:T(8,128)(2,1)} %all-gather.5.cloned.1.call-done, f32[128]{0:T(128)S(1)} %add_divide_fusion), kind=kLoop, calls=%fused_computation | loop fusion | flops 12582912 | bytes 16777728 | tf_op jit(solution)/shard_map/convert_element_type | solution.py:50
  839.0 6.1 slice_bitcast_fusion.1
  845.2 7.1 fusion
  852.3 16.9 %fusion.13 = f32[128,1,64,128]{3,0,2,1:T(8,128)S(1)} fusion(f32[128,128,2,64]{1,3,2,0:T(8,128)S(1)} %bitcast.19, f32[128,1,128]{2,0,1:T(8,128)S(1)} %get-tuple-element.11, f32[128,1,128]{2,0,1:T(8,128)S(1)} %get-tuple-element.12), kind=kOutput, calls=%fused_computation.16 | convolution fusion | flops 3221258240 | bytes 12713984 | tf_op jit(solution)/shard_map/fmps,fpk->msk/dot_general | solution.py:33
  869.2 4.4 copy.11
Async XLA Ops:
  6.5 798.2 %all-gather.7.cloned.1.call-start = ((), (), s32[]{:S(2)}) async-start(), calls=%async_computation.1 | async-start | bytes 4456448 | tf_op jit(solution)/shard_map/all_gather | solution.py:45
  7.3 807.8 %all-gather.5.cloned.1.call-start = ((), (), s32[]{:S(2)}) async-start(), calls=%async_computation | async-start | bytes 8650752 | tf_op jit(solution)/shard_map/all_gather | solution.py:48
Sparse Core Ops, SparseCore 0:
  9.4 107.3 all-gather.6
  120.0 111.7 all-gather.4
